TPU v7x, 128 devices: a whole 4x4x4 slice. The times are simulated.
128 devices in a mesh: row: 8 (over z, y_lo), col: 16 (over y_hi, x, core).
Axes of the slice: x: 4, y: 4 (y_hi: 2, y_lo: 2; y = y_hi * 2 + y_lo), z: 4, core: 2. Of those that a mesh axis runs over, the one named last changes fastest.
Arguments:
- features: bfloat16 [64, 128, 1024], P('row', 'col'), may hold values from -6 to 6
- gate_branch: bfloat16 [64, 128, 1024], P('row', 'col'), may hold values from -6 to 6
- w_row_proj: bfloat16 [1024, 128], replicated, may hold values from -0.1875 to 0.1875
- w_dt_row: bfloat16 [2, 32, 1024], P(None, None, 'col'), may hold values from -1 to 1
- dt_bias_row: float32 [2, 1024], P(None, 'col'), may hold values from -5 to -1
- rate_row: float32 [2, 1024, 16], P(None, 'col'), may hold values from 0.01 to 1
- skip_row: float32 [1024], P('col'), may hold values from 0.5 to 1.5
- conv_kernel: float32 [3, 3, 1024], P(None, None, 'col'), may hold values from -2 to 2
- conv_bias: float32 [1024], P('col'), may hold values from -3 to 3
- w_col_proj: bfloat16 [1024, 128], replicated, may hold values from -0.1875 to 0.1875
- w_dt_col: bfloat16 [2, 32, 1024], P(None, None, 'row'), may hold values from -1 to 1
- dt_bias_col: float32 [2, 1024], P(None, 'row'), may hold values from -5 to -1
- rate_col: float32 [2, 1024, 16], P(None, 'row'), may hold values from 0.01 to 1
Outputs:
- block_out: bfloat16 [64, 128, 1024], P(None, 'col', 'row')
All inputs are finite; a program needn't handle non-finite values.
Results may differ from a plain program's by a relative error of at most 0.0085.
The roundings to bfloat16 on the way count: a program that leaves them out, or rounds other values in their place, can miss the bound.
Values may be sent and summed in bfloat16 or wider, within the bound.
A program may use at most 64 MiB of HBM per device.

v0:
```python
import functools

import jax
import jax.numpy as jnp
from jax import lax
from jax.experimental import pallas as pl
from jax.experimental.pallas import tpu as pltpu
from jax.sharding import PartitionSpec as P

F32, BF16 = jnp.float32, jnp.bfloat16
MESH = pl.DeviceIdType.MESH
N = 16
LOG2E = 1.4426950408889634


def softplus(v):
    return jnp.maximum(v, 0.0) + jnp.log1p(jnp.exp(-jnp.abs(v)))


def silu(v):
    return v / (1.0 + jnp.exp(-v))


def turn(v):
    groups = v.shape[0] // 8
    return jnp.concatenate([v[8 * g : 8 * g + 8] for g in reversed(range(groups))], axis=0)


def swap(v):
    return pltpu.roll(v, 64, 1)


def dot(a, b):
    return jnp.dot(a, b, preferred_element_type=F32)


def scan_block(states, rows, step_ref, x_ref, bc_ref, bc_row, rates, emit):
    states = list(states)
    for row, brow in zip(rows, bc_row):
        step = step_ref[pl.ds(row, 8), :]
        drive = step * x_ref[pl.ds(row, 8), :]
        out = None
        for n in range(N):
            decay = jnp.exp2(step * rates[n])
            states[n] = decay * states[n] + drive * bc_ref[pl.ds(brow, 8), n * 128 : (n + 1) * 128]
            term = states[n] * bc_ref[pl.ds(brow, 8), (N + n) * 128 : (N + n + 1) * 128]
            out = term if out is None else out + term
        emit(row, out)
    return tuple(states)


def kernel(
    R, C,
    f_ref, g_ref, wrp_ref, wcp_ref, wd_ref, par_ref,
    out_ref,
    sx, rx, rp, sh, rh, s3, r3, s4, r4, rp4,
    sel, bc, step, x2, y2, sg, z, acc, hz,
    px_s, px_r, pp_s, pp_r, h_s, h_r, m_s, m_r, c_s, c_r, q_s, q_r,
):
    r, c = lax.axis_index("row"), lax.axis_index("col")
    half = C // 2
    TW = half * 8
    lane = lax.broadcasted_iota(jnp.int32, (1, 128), 1)
    low = lane < 64

    def col_copy(src, dst, ss, rs, slot_src, slot_dst, to):
        return pltpu.make_async_remote_copy(
            src_ref=src.at[slot_src], dst_ref=dst.at[slot_dst], send_sem=ss, recv_sem=rs,
            device_id={"col": to}, device_id_type=MESH)

    def row_copy(src, dst, ss, rs, slot_src, slot_dst, to):
        return pltpu.make_async_remote_copy(
            src_ref=src.at[slot_src], dst_ref=dst.at[slot_dst], send_sem=ss, recv_sem=rs,
            device_id={"row": to}, device_id_type=MESH)

    barrier = pltpu.get_barrier_semaphore()

    @pl.loop(1, C)
    def _(k):
        pl.semaphore_signal(barrier, inc=1, device_id={"col": lax.rem(c + k, C)}, device_id_type=MESH)

    @pl.loop(1, R)
    def _(k):
        pl.semaphore_signal(barrier, inc=1, device_id={"row": lax.rem(r + k, R)}, device_id_type=MESH)

    ta = lax.broadcasted_iota(jnp.int32, (64, 64), 0)
    tb = lax.broadcasted_iota(jnp.int32, (64, 64), 1)
    perm = jnp.where(tb == lax.rem(ta, 8) * 8 + lax.div(ta, 8), 1.0, 0.0).astype(BF16)

    proj = dot(f_ref[...], wrp_ref[...]).astype(BF16)
    rp[c] = dot(perm, proj).astype(BF16)

    pl.semaphore_wait(barrier, C - 1 + R - 1)

    @pl.loop(1, C)
    def _(k):
        to = lax.rem(c + k, C)
        col_copy(rp, rp, pp_s.at[to], pp_r.at[c], c, c, to).start()

    for j in range(half):
        fj = dot(perm, f_ref[:, 128 * j : 128 * j + 128])
        gj = dot(perm, g_ref[:, 128 * j : 128 * j + 128])
        sx[2 * j] = jnp.where(low, fj, swap(gj)).astype(BF16)
        sx[2 * j + 1] = jnp.where(low, swap(fj), gj).astype(BF16)

    @pl.loop(1, C)
    def _(k):
        to = lax.rem(c + k, C)
        col_copy(sx, rx, px_s.at[to], px_r.at[c], to, c, to).start()

    rx[c] = sx[c]

    kk = lax.broadcasted_iota(jnp.int32, (128, 128), 0)
    ll = lax.broadcasted_iota(jnp.int32, (128, 128), 1)
    kl = kk - jnp.where(ll >= 64, 64, 0)
    for n in range(2 * N):
        at = slice(n * 128, n * 128 + 128)
        sel[0, :, at] = jnp.where(kl == 32 + n, 1.0, 0.0).astype(BF16)
        sel[1, :, at] = jnp.where(kk == 32 + n, 1.0, 0.0).astype(BF16)
        sel[2, :, at] = jnp.where(kk == 96 + n, 1.0, 0.0).astype(BF16)

    base = jnp.where(c < half, c, C - 1 - c)

    @pl.loop(0, half)
    def _(k):
        b = lax.rem(base + k, half)
        o = C - 1 - b
        for s in (b, o):
            @pl.when(s != c)
            def _():
                col_copy(rp, rp, pp_s.at[s], pp_r.at[s], s, s, s).wait_recv()
        pb, po = rp[b].astype(F32), rp[o].astype(F32)
        for at, mine, other in ((b, pb, po), (o, po, pb)):
            src = jnp.where(low, mine, turn(other)).astype(BF16)
            rows = pl.ds(pl.multiple_of(at * 64, 64), 64)
            step[rows, :] = softplus(dot(src, wd_ref[:, 0:128]) + par_ref[0:1, :])
            for q in range(8):
                bc[rows, q * 512 : q * 512 + 512] = dot(src, sel[0, :, q * 512 : q * 512 + 512])

    @pl.loop(0, half)
    def _(k):
        b = lax.rem(base + k, half)
        o = C - 1 - b
        for s in (b, o):
            @pl.when(s != c)
            def _():
                col_copy(sx, rx, px_s.at[s], px_r.at[s], s, s, s).wait_recv()
        vb, vo = rx[b].astype(F32), rx[o].astype(F32)
        tb_, to_ = turn(vb), turn(vo)
        brow, orow = pl.ds(pl.multiple_of(b * 64, 64), 64), pl.ds(pl.multiple_of(o * 64, 64), 64)
        x2[brow, :] = jnp.where(low, vb, swap(to_))
        x2[orow, :] = jnp.where(low, vo, swap(tb_))
        sg[brow, :] = silu(jnp.where(low, swap(vb), to_))

    rates = [par_ref[16 + n : 17 + n, :] for n in range(N)]
    zero_states = tuple(jnp.zeros((8, 128), F32) for _ in range(N))

    def put(row, out):
        y2[pl.ds(row, 8), :] = out

    def row_body(i, states):
        rows = [pl.multiple_of(i * 64 + 8 * u, 8) for u in range(8)]
        return scan_block(states, rows, step, x2, bc, rows, rates, put)

    lax.fori_loop(0, C, row_body, zero_states)

    skip = par_ref[1:2, :]
    z[0:8, :] = jnp.zeros((8, 128), F32)
    for b in range(half):
        here, there = slice(64 * b, 64 * b + 64), slice(64 * (C - 1 - b), 64 * (C - b))
        mix = skip * x2[here, :] + y2[here, :] + swap(turn(y2[there, :]))
        gated = (mix * sg[here, :]).astype(BF16).astype(F32)
        z[64 * b + 8 : 64 * b + 72, :] = gated
    z[8 * TW + 8 : 8 * TW + 16, :] = swap(z[8 * TW : 8 * TW + 8, :])

    sh[0] = z[pl.ds(8 + 7, TW, stride=8), :].astype(BF16)
    sh[1] = z[pl.ds(8, TW, stride=8), :].astype(BF16)
    down = row_copy(sh, rh, h_s.at[0], h_r.at[0], 0, 0, lax.rem(r + 1, R))
    up = row_copy(sh, rh, h_s.at[1], h_r.at[1], 1, 1, lax.rem(r + R - 1, R))

    @pl.when(r < R - 1)
    def _():
        down.start()

    @pl.when(r > 0)
    def _():
        up.start()

    taps = [[par_ref[3 + 3 * i + j : 4 + 3 * i + j, :] for j in range(3)] for i in range(3)]
    sub = lax.broadcasted_iota(jnp.int32, (8, 128), 0)
    conv_bias = par_ref[2:3, :]

    @pl.loop(0, half)
    def _(b):
        group = [z[pl.ds(pl.multiple_of(b * 64 + 8 * u, 8), 8), :] for u in range(10)]
        for u in range(8):
            q = [taps[i][0] * group[u] + taps[i][1] * group[u + 1] + taps[i][2] * group[u + 2]
                 for i in range(3)]
            above = jnp.where(sub == 0, 0.0, pltpu.roll(q[0], 1, 0))
            below = jnp.where(sub == 7, 0.0, pltpu.roll(q[2], 7, 0))
            acc[pl.ds(pl.multiple_of(b * 64 + 8 * u, 8), 8), :] = conv_bias + above + q[1] + below

    @pl.when(r == 0)
    def _():
        rh[0] = jnp.zeros((TW, 128), BF16)

    @pl.when(r == R - 1)
    def _():
        rh[1] = jnp.zeros((TW, 128), BF16)

    @pl.when(r > 0)
    def _():
        down.wait_recv()

    @pl.when(r < R - 1)
    def _():
        up.wait_recv()

    for side, i, first in ((0, 0, 0), (1, 2, 7)):
        hz[0:8, :] = jnp.zeros((8, 128), F32)
        halo = rh[side].astype(F32)
        hz[8 : 8 + TW, :] = halo
        hz[8 + TW : 16 + TW, :] = swap(jnp.broadcast_to(halo[TW - 1 : TW, :], (8, 128)))
        add = (taps[i][0] * hz[7 : 7 + TW, :] + taps[i][1] * halo + taps[i][2] * hz[9 : 9 + TW, :])
        at = pl.ds(first, TW, stride=8)
        acc[at, :] = acc[at, :] + add

    for b in range(half):
        cells = silu(acc[64 * b : 64 * b + 64, :]).astype(BF16).astype(F32)
        near, far = cells[0:32, :], swap(turn(cells[32:64, :]))
        s3[b] = jnp.where(low, near, far).astype(BF16)
        s3[C - 1 - b] = jnp.where(low, far, near).astype(BF16)

    @pl.loop(1, C)
    def _(k):
        to = lax.rem(c + k, C)
        col_copy(s3, r3, m_s.at[to], m_r.at[c], to, c, to).start()

    r3[c] = s3[c]

    @pl.loop(0, C)
    def _(s):
        @pl.when(s != c)
        def _():
            col_copy(s3, r3, m_s.at[s], m_r.at[s], s, s, s).wait_recv()

    total = jnp.zeros((64, 128), F32)
    for j in range(R):
        one, two = r3[2 * j].astype(F32), r3[2 * j + 1].astype(F32)
        first = jnp.where(low, one, swap(two))
        second = jnp.where(low, swap(one), two)
        tokens = jnp.concatenate([first, turn(second)], axis=0).astype(BF16)
        tokens = dot(perm, tokens).astype(BF16)
        s4[j] = tokens
        total = total + dot(tokens, wcp_ref[128 * j : 128 * j + 128, :])
    rp4[r] = total.astype(BF16)

    @pl.loop(1, R)
    def _(k):
        to = lax.rem(r + k, R)
        row_copy(rp4, rp4, q_s.at[to], q_r.at[r], r, r, to).start()

    @pl.loop(1, R)
    def _(k):
        to = lax.rem(r + k, R)
        row_copy(s4, r4, c_s.at[to], c_r.at[r], to, r, to).start()

    r4[r] = s4[r]

    HT = 64 * R

    @pl.loop(0, R)
    def _(k):
        s = lax.rem(r + k, R)

        @pl.when(s != r)
        def _():
            row_copy(rp4, rp4, q_s.at[s], q_r.at[s], s, s, s).wait_recv()

        src = rp4[s]
        for d in range(2):
            rows = pl.ds(pl.multiple_of(d * HT + s * 64, 64), 64)
            raw = dot(src, wd_ref[:, 128 + 128 * d : 256 + 128 * d])
            step[rows, :] = softplus(raw + par_ref[12 + d : 13 + d, :])
            for q in range(8):
                bc[rows, q * 512 : q * 512 + 512] = dot(src, sel[1 + d, :, q * 512 : q * 512 + 512])

    @pl.loop(0, R)
    def _(k):
        s = lax.rem(r + k, R)

        @pl.when(s != r)
        def _():
            row_copy(s4, r4, c_s.at[s], c_r.at[s], s, s, s).wait_recv()

        cells = r4[s].astype(F32)
        for d in range(2):
            x2[pl.ds(pl.multiple_of(d * HT + s * 64, 64), 64), :] = cells

    for d in range(2):
        rates_d = [par_ref[32 + N * d + n : 33 + N * d + n, :] for n in range(N)]

        def col_body(i, states):
            block = i if d == 0 else R - 1 - i
            order = range(8) if d == 0 else range(7, -1, -1)
            rows = [pl.multiple_of(d * HT + block * 64 + 8 * u, 8) for u in order]
            return scan_block(states, rows, step, x2, bc, rows, rates_d, put)

        lax.fori_loop(0, R, col_body, zero_states)

    for b in range(R):
        out_ref[64 * b : 64 * b + 64, :] = (
            y2[64 * b : 64 * b + 64, :] + y2[HT + 64 * b : HT + 64 * b + 64, :]).astype(BF16)

    @pl.loop(1, C)
    def _(k):
        to = lax.rem(c + k, C)
        col_copy(rp, rp, pp_s.at[to], pp_r.at[c], c, c, to).wait_send()
        col_copy(sx, rx, px_s.at[to], px_r.at[c], to, c, to).wait_send()
        col_copy(s3, r3, m_s.at[to], m_r.at[c], to, c, to).wait_send()

    @pl.loop(1, R)
    def _(k):
        to = lax.rem(r + k, R)
        row_copy(rp4, rp4, q_s.at[to], q_r.at[r], r, r, to).wait_send()
        row_copy(s4, r4, c_s.at[to], c_r.at[r], to, r, to).wait_send()

    @pl.when(r < R - 1)
    def _():
        down.wait_send()

    @pl.when(r > 0)
    def _():
        up.wait_send()


def local(R, C, features, gate_branch, w_row_proj, w_dt_row, dt_bias_row, rate_row, skip_row,
          conv_kernel, conv_bias, w_col_proj, w_dt_col, dt_bias_col, rate_col):
    E = features.shape[2]
    both = lambda v: jnp.concatenate([v, v], axis=-1)
    flipped = conv_kernel[:, ::-1, :]
    params = jnp.concatenate(
        [
            dt_bias_row.reshape(1, 128),
            both(skip_row)[None],
            both(conv_bias)[None],
            jnp.concatenate([conv_kernel, flipped], axis=-1).reshape(9, 128),
            dt_bias_col,
            jnp.zeros((2, 128), F32),
            jnp.transpose(rate_row, (2, 0, 1)).reshape(N, 128) * -LOG2E,
            jnp.transpose(rate_col, (0, 2, 1)).reshape(2 * N, 128) * -LOG2E,
        ],
        axis=0,
    )
    zr = jnp.zeros((32, 64), BF16)
    wide = jnp.concatenate(
        [
            jnp.concatenate([w_dt_row[0], zr, w_dt_col[0], jnp.zeros((32, 128), BF16)], axis=1),
            jnp.zeros((32, 384), BF16),
            jnp.concatenate([zr, w_dt_row[1], jnp.zeros((32, 128), BF16), w_dt_col[1]], axis=1),
            jnp.zeros((32, 384), BF16),
        ],
        axis=0,
    )
    dma = pltpu.SemaphoreType.DMA
    TW = 4 * C
    out = pl.pallas_call(
        functools.partial(kernel, R, C),
        out_shape=jax.ShapeDtypeStruct((64 * R, 128), BF16),
        in_specs=[pl.BlockSpec(memory_space=pltpu.VMEM)] * 6,
        out_specs=pl.BlockSpec(memory_space=pltpu.VMEM),
        scratch_shapes=[
            pltpu.VMEM((C, 64, 128), BF16),
            pltpu.VMEM((C, 64, 128), BF16),
            pltpu.VMEM((C, 64, 128), BF16),
            pltpu.VMEM((2, TW, 128), BF16),
            pltpu.VMEM((2, TW, 128), BF16),
            pltpu.VMEM((C, 32, 128), BF16),
            pltpu.VMEM((C, 32, 128), BF16),
            pltpu.VMEM((R, 64, 128), BF16),
            pltpu.VMEM((R, 64, 128), BF16),
            pltpu.VMEM((R, 64, 128), BF16),
            pltpu.VMEM((3, 128, 4096), BF16),
            pltpu.VMEM((64 * C, 4096), F32),
            pltpu.VMEM((64 * C, 128), F32),
            pltpu.VMEM((64 * C, 128), F32),
            pltpu.VMEM((64 * C, 128), F32),
            pltpu.VMEM((32 * C, 128), F32),
            pltpu.VMEM((32 * C + 16, 128), F32),
            pltpu.VMEM((32 * C, 128), F32),
            pltpu.VMEM((TW + 16, 128), F32),
            dma((C,)), dma((C,)), dma((C,)), dma((C,)), dma((2,)), dma((2,)),
            dma((C,)), dma((C,)), dma((R,)), dma((R,)), dma((R,)), dma((R,)),
        ],
        compiler_params=pltpu.CompilerParams(
            collective_id=0, has_side_effects=True, vmem_limit_bytes=48 << 20),
    )(features.reshape(64, E), gate_branch.reshape(64, E), w_row_proj, w_col_proj, wide, params)
    return out.reshape(8 * R, 8, 128)


def solution(mesh):
    return jax.shard_map(
        functools.partial(local, mesh.shape["row"], mesh.shape["col"]),
        mesh=mesh,
        in_specs=(
            P("row", "col", None),
            P("row", "col", None),
            P(),
            P(None, None, "col"),
            P(None, "col"),
            P(None, "col", None),
            P("col"),
            P(None, None, "col"),
            P("col"),
            P(),
            P(None, None, "row"),
            P(None, "row"),
            P(None, "row", None),
        ),
        out_specs=P(None, "col", "row"),
        check_vma=False,
    )
```

profile of v0, /device:TPU:0, one launch (start us, length us, event | category | flops | bytes accessed | tf_op | source)
XLA Modules:
  0.0 46.4 jit_solution(4503949213705837113)
XLA Ops:
  0.0 0.0 copy-start.4
  0.0 0.8 %reshape.23 = f32[1,128]{1,0:T(1,128)S(1)} reshape(f32[2,64]{1,0:T(2,128)} %param.17) | data formatting | bytes 1024 | tf_op jit(solution)/shard_map/reshape | solution.py:344
  0.8 0.8 %maximum_bitcast_fusion = (f32[1,128]{1,0:T(1,128)S(1)}, f32[1,128]{1,0:T(1,128)S(1)}) fusion(f32[64]{0:T(128)} %param.19, f32[64]{0:T(128)} %param.21), kind=kLoop, calls=%fused_computation.8 | loop fusion | flops 256 | bytes 1536 | tf_op jit(solution)/shard_map/broadcast_in_dim | solution.py:345
  1.6 0.0 copy-start.5
  1.6 0.0 copy-done.4
  1.6 0.0 copy-start
  1.6 0.0 copy-start.1
  1.6 0.1 pad_maximum_fusion.1
  1.7 0.8 %multiply_bitcast_fusion = f32[16,2,64]{2,0,1:T(8,128)S(1)} fusion(f32[2,64,16]{1,2,0:T(8,128)} %param.18), kind=kLoop, calls=%fused_computation.1 | loop fusion | flops 2048 | bytes 16384 | tf_op jit(solution)/shard_map/mul | solution.py:350
  2.5 0.1 mul.27
  2.6 0.7 %broadcast_multiply_fusion = f32[2,128,16]{1,2,0:T(8,128)S(1)} fusion(f32[2,128,16]{1,2,0:T(8,128)} %param.25), kind=kLoop, calls=%fused_computation.2 | loop fusion | flops 4096 | bytes 32768 | tf_op jit(solution)/shard_map/mul | solution.py:351
  3.3 0.0 copy-done.5
  3.3 0.1 concatenate.27.par_ref
  3.4 0.7 %slice_bitcast_fusion.3 = (bf16[32,64]{1,0:T(8,128)(2,1)S(1)}, bf16[32,64]{1,0:T(8,128)(2,1)S(1)}) fusion(bf16[2,32,64]{2,1,0:T(8,128)(2,1)} %param.16), kind=kLoop, calls=%fused_computation.6 | loop fusion | bytes 16384 | tf_op jit(solution)/shard_map/squeeze | solution.py:358
  4.2 0.7 %slice_bitcast_fusion.2 = (bf16[32,128]{1,0:T(8,128)(2,1)S(1)}, bf16[32,128]{1,0:T(8,128)(2,1)S(1)}) fusion(bf16[2,32,128]{2,1,0:T(8,128)(2,1)} %param.23), kind=kLoop, calls=%fused_computation.5 | loop fusion | bytes 32768 | tf_op jit(solution)/shard_map/squeeze | solution.py:358
  4.9 0.1 pad_maximum_fusion.wd_ref
  5.0 0.0 copy-done
  5.0 0.0 copy-done.1
  5.0 0.0 copy-start.2
  5.0 0.9 %copy-done.2 = bf16[8,8,1024]{2,1,0:T(8,128)(2,1)S(1)} copy-done((bf16[8,8,1024]{2,1,0:T(8,128)(2,1)S(1)}, bf16[8,8,1024]{2,1,0:T(8,128)(2,1)}, u32[]{:S(2)}) %copy-start.2) | copy-done | bytes 131096
  5.9 0.0 copy-start.3
  5.9 0.9 %copy-done.3 = bf16[8,8,1024]{2,1,0:T(8,128)(2,1)S(1)} copy-done((bf16[8,8,1024]{2,1,0:T(8,128)(2,1)S(1)}, bf16[8,8,1024]{2,1,0:T(8,128)(2,1)}, u32[]{:S(2)}) %copy-start.3) | copy-done | bytes 131096
  6.8 38.9 %shard_map.127 = bf16[512,128]{1,0:T(8,128)(2,1)S(1)} custom-call(bf16[64,1024]{1,0:T(8,128)(2,1)S(1)} %bitcast.21, bf16[64,1024]{1,0:T(8,128)(2,1)S(1)} %bitcast.22, bf16[1024,128]{1,0:T(8,128)(2,1)S(1)} %copy-done, bf16[1024,128]{1,0:T(8,128)(2,1)S(1)} %copy-done.1, bf16[128,384]{1,0:T(8,128)(2,1)S(1)} %pad_maximum_fusion.wd_ref, ...), custom_call_target="tpu_custom_call" | custom-call | tf_op jit(solution)/shard_map/pallas_call | solution.py:367
  45.7 0.7 %copy.16 = bf16[64,8,128]{2,1,0:T(8,128)(2,1)} copy(bf16[64,8,128]{2,1,0:T(8,128)(2,1)S(1)} %bitcast.20) | data formatting | bytes 262144
  (7 shorter events, 0.1 us)
Async XLA Ops:
  0.0 1.6 %copy-start.4 = (f32[3,3,64]{2,1,0:T(4,128)S(1)}, f32[3,3,64]{2,1,0:T(4,128)}, u32[]{:S(2)}) copy-start(f32[3,3,64]{2,1,0:T(4,128)} %param.20) | copy-start | bytes 6916
  1.6 1.7 %copy-start.5 = (f32[2,128]{1,0:T(2,128)S(1)}, f32[2,128]{1,0:T(2,128)}, u32[]{:S(2)}) copy-start(f32[2,128]{1,0:T(2,128)} %param.24) | copy-start | bytes 3076
  1.6 3.4 %copy-start = (bf16[1024,128]{1,0:T(8,128)(2,1)S(1)}, bf16[1024,128]{1,0:T(8,128)(2,1)}, u32[]{:S(2)}) copy-start(bf16[1024,128]{1,0:T(8,128)(2,1)} %wrp_ref.1) | copy-start | bytes 786436
  1.6 3.4 %copy-start.1 = (bf16[1024,128]{1,0:T(8,128)(2,1)S(1)}, bf16[1024,128]{1,0:T(8,128)(2,1)}, u32[]{:S(2)}) copy-start(bf16[1024,128]{1,0:T(8,128)(2,1)} %wcp_ref.1) | copy-start | bytes 786436
  5.0 0.9 %copy-start.2 = (bf16[8,8,1024]{2,1,0:T(8,128)(2,1)S(1)}, bf16[8,8,1024]{2,1,0:T(8,128)(2,1)}, u32[]{:S(2)}) copy-start(bf16[8,8,1024]{2,1,0:T(8,128)(2,1)} %param.13) | copy-start | bytes 393220
  5.9 0.9 %copy-start.3 = (bf16[8,8,1024]{2,1,0:T(8,128)(2,1)S(1)}, bf16[8,8,1024]{2,1,0:T(8,128)(2,1)}, u32[]{:S(2)}) copy-start(bf16[8,8,1024]{2,1,0:T(8,128)(2,1)} %param.14) | copy-start | bytes 393220
where the time goes:
time: 46.9 us; the launch traced here: 46.4 us
  Pallas kernels  38.9 us (83%)
  local copies, waits for them, and re-layouts  4.96 us (11%)
  other arithmetic  2.45 us (5%)
    pallas_call x1, Pallas kernels, local(): pl.pallas_call(functools.partial(kernel, R, C), out_shape=jax.ShapeDtypeS...  38.9 us
    unnamed x13, local copies, waits for them, and re-layouts  2.48 us

commit v1 on v0

--- a/solution.py
+++ b/solution.py
@@ -51,8 +51,11 @@
 
 def kernel(
     R, C,
-    f_ref, g_ref, wrp_ref, wcp_ref, wd_ref, par_ref,
+    f_hbm, g_hbm, wrp_hbm, wdtr_hbm, biasr_hbm, rater_hbm, skip_hbm, kern_hbm, biask_hbm, wcp_hbm,
+    wdtc_hbm, biasc_hbm, ratec_hbm,
     out_ref,
+    f_ref, g_ref, wrp_ref, wdtr, biasr, rater, skipr, kern, biask, wcp_ref, wdtc, biasc, ratec,
+    wd_ref, load_sem,
     sx, rx, rp, sh, rh, s3, r3, s4, r4, rp4,
     sel, bc, step, x2, y2, sg, z, acc, hz,
     px_s, px_r, pp_s, pp_r, h_s, h_r, m_s, m_r, c_s, c_r, q_s, q_r,
@@ -73,6 +76,51 @@
             src_ref=src.at[slot_src], dst_ref=dst.at[slot_dst], send_sem=ss, recv_sem=rs,
             device_id={"row": to}, device_id_type=MESH)
 
+    sources = (f_hbm, wrp_hbm, g_hbm, wdtr_hbm, biasr_hbm, rater_hbm, skip_hbm, kern_hbm, biask_hbm,
+               wcp_hbm, wdtc_hbm, biasc_hbm, ratec_hbm)
+    targets = (f_ref, wrp_ref, g_ref, wdtr, biasr, rater, skipr, kern, biask,
+               wcp_ref, wdtc, biasc, ratec)
+    loads = [pltpu.make_async_copy(a, b, load_sem.at[i])
+             for i, (a, b) in enumerate(zip(sources, targets))]
+    for load in loads:
+        load.start()
+
+    sent = []
+
+    def finish():
+        for wait in sent:
+            wait()
+
+    def to_col(src, dst, ss, rs, own):
+        def copy(k):
+            to = lax.rem(c + k, C)
+            return col_copy(src, dst, ss.at[to], rs.at[c], c if own else to, c, to)
+
+        @pl.loop(1, C)
+        def _(k):
+            copy(k).start()
+
+        @sent.append
+        def _():
+            @pl.loop(1, C)
+            def _(k):
+                copy(k).wait_send()
+
+    def to_row(src, dst, ss, rs, own):
+        def copy(k):
+            to = lax.rem(r + k, R)
+            return row_copy(src, dst, ss.at[to], rs.at[r], r if own else to, r, to)
+
+        @pl.loop(1, R)
+        def _(k):
+            copy(k).start()
+
+        @sent.append
+        def _():
+            @pl.loop(1, R)
+            def _(k):
+                copy(k).wait_send()
+
     barrier = pltpu.get_barrier_semaphore()
 
     @pl.loop(1, C)
@@ -87,26 +135,23 @@
     tb = lax.broadcasted_iota(jnp.int32, (64, 64), 1)
     perm = jnp.where(tb == lax.rem(ta, 8) * 8 + lax.div(ta, 8), 1.0, 0.0).astype(BF16)
 
+    loads[0].wait()
+    loads[1].wait()
     proj = dot(f_ref[...], wrp_ref[...]).astype(BF16)
     rp[c] = dot(perm, proj).astype(BF16)
 
     pl.semaphore_wait(barrier, C - 1 + R - 1)
 
-    @pl.loop(1, C)
-    def _(k):
-        to = lax.rem(c + k, C)
-        col_copy(rp, rp, pp_s.at[to], pp_r.at[c], c, c, to).start()
-
+    to_col(rp, rp, pp_s, pp_r, True)
+
+    loads[2].wait()
     for j in range(half):
         fj = dot(perm, f_ref[:, 128 * j : 128 * j + 128])
         gj = dot(perm, g_ref[:, 128 * j : 128 * j + 128])
         sx[2 * j] = jnp.where(low, fj, swap(gj)).astype(BF16)
         sx[2 * j + 1] = jnp.where(low, swap(fj), gj).astype(BF16)
 
-    @pl.loop(1, C)
-    def _(k):
-        to = lax.rem(c + k, C)
-        col_copy(sx, rx, px_s.at[to], px_r.at[c], to, c, to).start()
+    to_col(sx, rx, px_s, px_r, False)
 
     rx[c] = sx[c]
 
@@ -118,6 +163,25 @@
         sel[0, :, at] = jnp.where(kl == 32 + n, 1.0, 0.0).astype(BF16)
         sel[1, :, at] = jnp.where(kk == 32 + n, 1.0, 0.0).astype(BF16)
         sel[2, :, at] = jnp.where(kk == 96 + n, 1.0, 0.0).astype(BF16)
+
+    for load in loads[3:]:
+        load.wait()
+    ea = lax.broadcasted_iota(jnp.int32, (64, 128), 0)
+    eb = lax.broadcasted_iota(jnp.int32, (64, 128), 1)
+    wd_ref[...] = jnp.zeros((128, 384), BF16)
+    wd_ref[0:32, 0:128] = dot(wdtr[0], jnp.where(ea == eb, 1.0, 0.0).astype(BF16)).astype(BF16)
+    wd_ref[64:96, 0:128] = dot(wdtr[1], jnp.where(ea == eb - 64, 1.0, 0.0).astype(BF16)).astype(BF16)
+    wd_ref[0:32, 128:256] = wdtc[0]
+    wd_ref[64:96, 256:384] = wdtc[1]
+
+    def beside(a, b):
+        return jnp.concatenate([a, b], axis=1)
+
+    bias_row = beside(biasr[0:1, :], biasr[1:2, :])
+    skip = beside(skipr[...], skipr[...])
+    conv_bias = beside(biask[...], biask[...])
+    taps = [[beside(kern[i, j : j + 1, :], kern[i, 2 - j : 3 - j, :]) for j in range(3)] for i in range(3)]
+    rate_all = beside(rater[0], rater[1]) * -LOG2E
 
     base = jnp.where(c < half, c, C - 1 - c)
 
@@ -133,7 +197,7 @@
         for at, mine, other in ((b, pb, po), (o, po, pb)):
             src = jnp.where(low, mine, turn(other)).astype(BF16)
             rows = pl.ds(pl.multiple_of(at * 64, 64), 64)
-            step[rows, :] = softplus(dot(src, wd_ref[:, 0:128]) + par_ref[0:1, :])
+            step[rows, :] = softplus(dot(src, wd_ref[:, 0:128]) + bias_row)
             for q in range(8):
                 bc[rows, q * 512 : q * 512 + 512] = dot(src, sel[0, :, q * 512 : q * 512 + 512])
 
@@ -152,7 +216,7 @@
         x2[orow, :] = jnp.where(low, vo, swap(tb_))
         sg[brow, :] = silu(jnp.where(low, swap(vb), to_))
 
-    rates = [par_ref[16 + n : 17 + n, :] for n in range(N)]
+    rates = [rate_all[n : n + 1, :] for n in range(N)]
     zero_states = tuple(jnp.zeros((8, 128), F32) for _ in range(N))
 
     def put(row, out):
@@ -164,7 +228,6 @@
 
     lax.fori_loop(0, C, row_body, zero_states)
 
-    skip = par_ref[1:2, :]
     z[0:8, :] = jnp.zeros((8, 128), F32)
     for b in range(half):
         here, there = slice(64 * b, 64 * b + 64), slice(64 * (C - 1 - b), 64 * (C - b))
@@ -186,9 +249,17 @@
     def _():
         up.start()
 
-    taps = [[par_ref[3 + 3 * i + j : 4 + 3 * i + j, :] for j in range(3)] for i in range(3)]
+    @sent.append
+    def _():
+        @pl.when(r < R - 1)
+        def _():
+            down.wait_send()
+
+        @pl.when(r > 0)
+        def _():
+            up.wait_send()
+
     sub = lax.broadcasted_iota(jnp.int32, (8, 128), 0)
-    conv_bias = par_ref[2:3, :]
 
     @pl.loop(0, half)
     def _(b):
@@ -231,10 +302,7 @@
         s3[b] = jnp.where(low, near, far).astype(BF16)
         s3[C - 1 - b] = jnp.where(low, far, near).astype(BF16)
 
-    @pl.loop(1, C)
-    def _(k):
-        to = lax.rem(c + k, C)
-        col_copy(s3, r3, m_s.at[to], m_r.at[c], to, c, to).start()
+    to_col(s3, r3, m_s, m_r, False)
 
     r3[c] = s3[c]
 
@@ -255,15 +323,9 @@
         total = total + dot(tokens, wcp_ref[128 * j : 128 * j + 128, :])
     rp4[r] = total.astype(BF16)
 
-    @pl.loop(1, R)
-    def _(k):
-        to = lax.rem(r + k, R)
-        row_copy(rp4, rp4, q_s.at[to], q_r.at[r], r, r, to).start()
-
-    @pl.loop(1, R)
-    def _(k):
-        to = lax.rem(r + k, R)
-        row_copy(s4, r4, c_s.at[to], c_r.at[r], to, r, to).start()
+    to_row(rp4, rp4, q_s, q_r, True)
+
+    to_row(s4, r4, c_s, c_r, False)
 
     r4[r] = s4[r]
 
@@ -281,7 +343,7 @@
         for d in range(2):
             rows = pl.ds(pl.multiple_of(d * HT + s * 64, 64), 64)
             raw = dot(src, wd_ref[:, 128 + 128 * d : 256 + 128 * d])
-            step[rows, :] = softplus(raw + par_ref[12 + d : 13 + d, :])
+            step[rows, :] = softplus(raw + biasc[d : d + 1, :])
             for q in range(8):
                 bc[rows, q * 512 : q * 512 + 512] = dot(src, sel[1 + d, :, q * 512 : q * 512 + 512])
 
@@ -298,7 +360,8 @@
             x2[pl.ds(pl.multiple_of(d * HT + s * 64, 64), 64), :] = cells
 
     for d in range(2):
-        rates_d = [par_ref[32 + N * d + n : 33 + N * d + n, :] for n in range(N)]
+        rate_d = ratec[d] * -LOG2E
+        rates_d = [rate_d[n : n + 1, :] for n in range(N)]
 
         def col_body(i, states):
             block = i if d == 0 else R - 1 - i
@@ -312,64 +375,35 @@
         out_ref[64 * b : 64 * b + 64, :] = (
             y2[64 * b : 64 * b + 64, :] + y2[HT + 64 * b : HT + 64 * b + 64, :]).astype(BF16)
 
-    @pl.loop(1, C)
-    def _(k):
-        to = lax.rem(c + k, C)
-        col_copy(rp, rp, pp_s.at[to], pp_r.at[c], c, c, to).wait_send()
-        col_copy(sx, rx, px_s.at[to], px_r.at[c], to, c, to).wait_send()
-        col_copy(s3, r3, m_s.at[to], m_r.at[c], to, c, to).wait_send()
-
-    @pl.loop(1, R)
-    def _(k):
-        to = lax.rem(r + k, R)
-        row_copy(rp4, rp4, q_s.at[to], q_r.at[r], r, r, to).wait_send()
-        row_copy(s4, r4, c_s.at[to], c_r.at[r], to, r, to).wait_send()
-
-    @pl.when(r < R - 1)
-    def _():
-        down.wait_send()
-
-    @pl.when(r > 0)
-    def _():
-        up.wait_send()
+    finish()
 
 
 def local(R, C, features, gate_branch, w_row_proj, w_dt_row, dt_bias_row, rate_row, skip_row,
           conv_kernel, conv_bias, w_col_proj, w_dt_col, dt_bias_col, rate_col):
     E = features.shape[2]
-    both = lambda v: jnp.concatenate([v, v], axis=-1)
-    flipped = conv_kernel[:, ::-1, :]
-    params = jnp.concatenate(
-        [
-            dt_bias_row.reshape(1, 128),
-            both(skip_row)[None],
-            both(conv_bias)[None],
-            jnp.concatenate([conv_kernel, flipped], axis=-1).reshape(9, 128),
-            dt_bias_col,
-            jnp.zeros((2, 128), F32),
-            jnp.transpose(rate_row, (2, 0, 1)).reshape(N, 128) * -LOG2E,
-            jnp.transpose(rate_col, (0, 2, 1)).reshape(2 * N, 128) * -LOG2E,
-        ],
-        axis=0,
-    )
-    zr = jnp.zeros((32, 64), BF16)
-    wide = jnp.concatenate(
-        [
-            jnp.concatenate([w_dt_row[0], zr, w_dt_col[0], jnp.zeros((32, 128), BF16)], axis=1),
-            jnp.zeros((32, 384), BF16),
-            jnp.concatenate([zr, w_dt_row[1], jnp.zeros((32, 128), BF16), w_dt_col[1]], axis=1),
-            jnp.zeros((32, 384), BF16),
-        ],
-        axis=0,
-    )
     dma = pltpu.SemaphoreType.DMA
     TW = 4 * C
     out = pl.pallas_call(
         functools.partial(kernel, R, C),
         out_shape=jax.ShapeDtypeStruct((64 * R, 128), BF16),
-        in_specs=[pl.BlockSpec(memory_space=pltpu.VMEM)] * 6,
+        in_specs=[pl.BlockSpec(memory_space=pltpu.HBM)] * 13,
         out_specs=pl.BlockSpec(memory_space=pltpu.VMEM),
         scratch_shapes=[
+            pltpu.VMEM((64, E), BF16),
+            pltpu.VMEM((64, E), BF16),
+            pltpu.VMEM((E, 128), BF16),
+            pltpu.VMEM((2, 32, 64), BF16),
+            pltpu.VMEM((2, 64), F32),
+            pltpu.VMEM((2, N, 64), F32),
+            pltpu.VMEM((1, 64), F32),
+            pltpu.VMEM((3, 3, 64), F32),
+            pltpu.VMEM((1, 64), F32),
+            pltpu.VMEM((E, 128), BF16),
+            pltpu.VMEM((2, 32, 128), BF16),
+            pltpu.VMEM((2, 128), F32),
+            pltpu.VMEM((2, N, 128), F32),
+            pltpu.VMEM((128, 384), BF16),
+            dma((13,)),
             pltpu.VMEM((C, 64, 128), BF16),
             pltpu.VMEM((C, 64, 128), BF16),
             pltpu.VMEM((C, 64, 128), BF16),
@@ -393,8 +427,10 @@
             dma((C,)), dma((C,)), dma((R,)), dma((R,)), dma((R,)), dma((R,)),
         ],
         compiler_params=pltpu.CompilerParams(
-            collective_id=0, has_side_effects=True, vmem_limit_bytes=48 << 20),
-    )(features.reshape(64, E), gate_branch.reshape(64, E), w_row_proj, w_col_proj, wide, params)
+            collective_id=0, has_side_effects=True, vmem_limit_bytes=63 << 20),
+    )(features.reshape(64, E), gate_branch.reshape(64, E), w_row_proj, w_dt_row, dt_bias_row,
+      jnp.transpose(rate_row, (0, 2, 1)), skip_row.reshape(1, 64), conv_kernel,
+      conv_bias.reshape(1, 64), w_col_proj, w_dt_col, dt_bias_col, jnp.transpose(rate_col, (0, 2, 1)))
     return out.reshape(8 * R, 8, 128)
 
 

time: 46.9 us -> 41.8 us (0.89)
  local copies, waits for them, and re-layouts: 4.96 us -> 1.57 us
  other arithmetic: 2.45 us -> 0 us
  Pallas kernels: 38.9 us -> 40.1 us
    mul x2 -> x0, other arithmetic: 1.48 us -> none  [the longest x1 0.76 us: local(): jnp.transpose(rate_row, (2, 0, 1)).reshape(N, 128) * -LOG2E]
    squeeze x2 -> x0, local copies, waits for them, and re-layouts: 1.43 us -> none  [the longest x1 0.72 us: local(): w_dt_row[0]]
    pallas_call x1, Pallas kernels: 38.9 us -> 40.1 us  [local(): pl.pallas_call(functools.partial(kernel, R, C), out_shape=jax.ShapeDtypeS...]
    unnamed x13 -> x1, local copies, waits for them, and re-layouts: 2.48 us -> 1.57 us
    broadcast_in_dim x1 -> x0, other arithmetic: 0.81 us -> none  [local(): both(skip_row)[None]]
    reshape x2 -> x0, local copies, waits for them, and re-layouts: 0.78 us -> none  [the longest x1 0.77 us: local(): dt_bias_row.reshape(1, 128)]
where the time goes in v1:
time: 41.8 us; the launch traced here: 41.7 us
  Pallas kernels  40.1 us (96%)
  local copies, waits for them, and re-layouts  1.57 us (4%)
    pallas_call x1, Pallas kernels, local(): pl.pallas_call(functools.partial(kernel, R, C), out_shape=jax.ShapeDtypeS...  40.1 us
    unnamed x1, local copies, waits for them, and re-layouts  1.57 us

profile of v1, /device:TPU:0, one launch (start us, length us, event | category | flops | bytes accessed | tf_op | source)
XLA Modules:
  0.0 41.7 jit_solution(12942658655905449066)
XLA Ops:
  0.0 40.1 %shard_map.127 = bf16[512,128]{1,0:T(8,128)(2,1)} custom-call(bf16[64,1024]{1,0:T(8,128)(2,1)} %bitcast.8, bf16[64,1024]{1,0:T(8,128)(2,1)} %bitcast.9, bf16[1024,128]{1,0:T(8,128)(2,1)} %wrp_hbm.1, bf16[2,32,64]{2,1,0:T(8,128)(2,1)} %wdtr_hbm.1, f32[2,64]{1,0:T(2,128)} %biasr_hbm.1, f32[2,16,64]{2,1,0:T(8,128)} %bitcast.10, f32[1,64]{1,0:T(1,128)} %bitcast.12, ...), custom_call_target="tpu_custom_call" | custom-call | tf_op jit(solution)/shard_map/pallas_call | solution.py:386
  40.1 1.6 %copy.15 = bf16[64,8,128]{2,1,0:T(8,128)(2,1)} copy(bf16[64,8,128]{2,1,0:T(8,128)(2,1)} %bitcast.7) | data formatting | bytes 262144

commit v2 on v1

--- a/solution.py
+++ b/solution.py
@@ -34,16 +34,16 @@
     return jnp.dot(a, b, preferred_element_type=F32)
 
 
-def scan_block(states, rows, step_ref, x_ref, bc_ref, bc_row, rates, emit):
+def scan_block(states, rows, x_rows, step_ref, x_ref, bc_ref, rates, emit):
     states = list(states)
-    for row, brow in zip(rows, bc_row):
+    for row, x_row in zip(rows, x_rows):
         step = step_ref[pl.ds(row, 8), :]
-        drive = step * x_ref[pl.ds(row, 8), :]
+        drive = step * x_ref[pl.ds(x_row, 8), :]
         out = None
         for n in range(N):
             decay = jnp.exp2(step * rates[n])
-            states[n] = decay * states[n] + drive * bc_ref[pl.ds(brow, 8), n * 128 : (n + 1) * 128]
-            term = states[n] * bc_ref[pl.ds(brow, 8), (N + n) * 128 : (N + n + 1) * 128]
+            states[n] = decay * states[n] + drive * bc_ref[pl.ds(row, 8), n * 128 : (n + 1) * 128]
+            term = states[n] * bc_ref[pl.ds(row, 8), (N + n) * 128 : (N + n + 1) * 128]
             out = term if out is None else out + term
         emit(row, out)
     return tuple(states)
@@ -56,7 +56,7 @@
     out_ref,
     f_ref, g_ref, wrp_ref, wdtr, biasr, rater, skipr, kern, biask, wcp_ref, wdtc, biasc, ratec,
     wd_ref, load_sem,
-    sx, rx, rp, sh, rh, s3, r3, s4, r4, rp4,
+    sx, rx, rp, sh, rh, s3, r3, tok, s4, r4, rp4,
     sel, bc, step, x2, y2, sg, z, acc, hz,
     px_s, px_r, pp_s, pp_r, h_s, h_r, m_s, m_r, c_s, c_r, q_s, q_r,
 ):
@@ -76,60 +76,38 @@
             src_ref=src.at[slot_src], dst_ref=dst.at[slot_dst], send_sem=ss, recv_sem=rs,
             device_id={"row": to}, device_id_type=MESH)
 
+    def send(axis, src, dst, ss, rs, own):
+        me, size = (c, C) if axis == "col" else (r, R)
+        for k in range(1, size):
+            to = lax.rem(me + k, size)
+            pltpu.make_async_remote_copy(
+                src_ref=src.at[me if own else to], dst_ref=dst.at[me], send_sem=ss, recv_sem=rs,
+                device_id={axis: to}, device_id_type=MESH).start()
+
+    def every(axis, ref, ss, rs):
+        me, size = (c, C) if axis == "col" else (r, R)
+        some = ref.at[pl.ds(0, size - 1)]
+        return pltpu.make_async_remote_copy(
+            src_ref=some, dst_ref=some, send_sem=ss, recv_sem=rs,
+            device_id={axis: lax.rem(me + 1, size)}, device_id_type=MESH)
+
     sources = (f_hbm, wrp_hbm, g_hbm, wdtr_hbm, biasr_hbm, rater_hbm, skip_hbm, kern_hbm, biask_hbm,
                wcp_hbm, wdtc_hbm, biasc_hbm, ratec_hbm)
     targets = (f_ref, wrp_ref, g_ref, wdtr, biasr, rater, skipr, kern, biask,
                wcp_ref, wdtc, biasc, ratec)
     loads = [pltpu.make_async_copy(a, b, load_sem.at[i])
              for i, (a, b) in enumerate(zip(sources, targets))]
-    for load in loads:
+    for load in loads[:3]:
         load.start()
 
-    sent = []
-
-    def finish():
-        for wait in sent:
-            wait()
-
-    def to_col(src, dst, ss, rs, own):
-        def copy(k):
-            to = lax.rem(c + k, C)
-            return col_copy(src, dst, ss.at[to], rs.at[c], c if own else to, c, to)
-
-        @pl.loop(1, C)
-        def _(k):
-            copy(k).start()
-
-        @sent.append
-        def _():
-            @pl.loop(1, C)
-            def _(k):
-                copy(k).wait_send()
-
-    def to_row(src, dst, ss, rs, own):
-        def copy(k):
-            to = lax.rem(r + k, R)
-            return row_copy(src, dst, ss.at[to], rs.at[r], r if own else to, r, to)
-
-        @pl.loop(1, R)
-        def _(k):
-            copy(k).start()
-
-        @sent.append
-        def _():
-            @pl.loop(1, R)
-            def _(k):
-                copy(k).wait_send()
-
     barrier = pltpu.get_barrier_semaphore()
-
-    @pl.loop(1, C)
-    def _(k):
+    for k in range(1, C):
         pl.semaphore_signal(barrier, inc=1, device_id={"col": lax.rem(c + k, C)}, device_id_type=MESH)
-
-    @pl.loop(1, R)
-    def _(k):
+    for k in range(1, R):
         pl.semaphore_signal(barrier, inc=1, device_id={"row": lax.rem(r + k, R)}, device_id_type=MESH)
+
+    for load in loads[3:]:
+        load.start()
 
     ta = lax.broadcasted_iota(jnp.int32, (64, 64), 0)
     tb = lax.broadcasted_iota(jnp.int32, (64, 64), 1)
@@ -139,10 +117,6 @@
     loads[1].wait()
     proj = dot(f_ref[...], wrp_ref[...]).astype(BF16)
     rp[c] = dot(perm, proj).astype(BF16)
-
-    pl.semaphore_wait(barrier, C - 1 + R - 1)
-
-    to_col(rp, rp, pp_s, pp_r, True)
 
     loads[2].wait()
     for j in range(half):
@@ -151,8 +125,11 @@
         sx[2 * j] = jnp.where(low, fj, swap(gj)).astype(BF16)
         sx[2 * j + 1] = jnp.where(low, swap(fj), gj).astype(BF16)
 
-    to_col(sx, rx, px_s, px_r, False)
-
+    pl.semaphore_wait(barrier, C - 1 + R - 1)
+    for k in range(1, C):
+        to = lax.rem(c + k, C)
+        col_copy(rp, rp, pp_s, pp_r.at[c], c, c, to).start()
+    send("col", sx, rx, px_s, px_r, False)
     rx[c] = sx[c]
 
     kk = lax.broadcasted_iota(jnp.int32, (128, 128), 0)
@@ -184,37 +161,36 @@
     rate_all = beside(rater[0], rater[1]) * -LOG2E
 
     base = jnp.where(c < half, c, C - 1 - c)
-
-    @pl.loop(0, half)
+    first = lax.div(base, 2)
+
+    @pl.loop(0, half // 2)
     def _(k):
-        b = lax.rem(base + k, half)
-        o = C - 1 - b
-        for s in (b, o):
+        b = lax.rem(first + k, half // 2) * 2
+        blocks = (b, b + 1, C - 2 - b, C - 1 - b)
+        for s in blocks:
             @pl.when(s != c)
             def _():
-                col_copy(rp, rp, pp_s.at[s], pp_r.at[s], s, s, s).wait_recv()
-        pb, po = rp[b].astype(F32), rp[o].astype(F32)
-        for at, mine, other in ((b, pb, po), (o, po, pb)):
-            src = jnp.where(low, mine, turn(other)).astype(BF16)
-            rows = pl.ds(pl.multiple_of(at * 64, 64), 64)
-            step[rows, :] = softplus(dot(src, wd_ref[:, 0:128]) + bias_row)
-            for q in range(8):
-                bc[rows, q * 512 : q * 512 + 512] = dot(src, sel[0, :, q * 512 : q * 512 + 512])
-
-    @pl.loop(0, half)
-    def _(k):
-        b = lax.rem(base + k, half)
+                col_copy(rp, rp, pp_s, pp_r.at[s], s, s, s).wait_recv()
+        projs = [rp[s].astype(F32) for s in blocks]
+        src = jnp.concatenate(
+            [jnp.where(low, projs[i], turn(projs[3 - i])) for i in range(4)], axis=0).astype(BF16)
+        rows = [pl.ds(pl.multiple_of(s * 64, 64), 64) for s in blocks]
+        steps = softplus(dot(src, wd_ref[:, 0:128]) + bias_row)
+        for i in range(4):
+            step[rows[i], :] = steps[64 * i : 64 * i + 64, :]
+        for q in range(8):
+            spread = dot(src, sel[0, :, q * 512 : q * 512 + 512])
+            for i in range(4):
+                bc[rows[i], q * 512 : q * 512 + 512] = spread[64 * i : 64 * i + 64, :]
+
+    every("col", rx, px_s, px_r).wait_recv()
+    for b in range(half):
         o = C - 1 - b
-        for s in (b, o):
-            @pl.when(s != c)
-            def _():
-                col_copy(sx, rx, px_s.at[s], px_r.at[s], s, s, s).wait_recv()
         vb, vo = rx[b].astype(F32), rx[o].astype(F32)
         tb_, to_ = turn(vb), turn(vo)
-        brow, orow = pl.ds(pl.multiple_of(b * 64, 64), 64), pl.ds(pl.multiple_of(o * 64, 64), 64)
-        x2[brow, :] = jnp.where(low, vb, swap(to_))
-        x2[orow, :] = jnp.where(low, vo, swap(tb_))
-        sg[brow, :] = silu(jnp.where(low, swap(vb), to_))
+        x2[64 * b : 64 * b + 64, :] = jnp.where(low, vb, swap(to_))
+        x2[64 * o : 64 * o + 64, :] = jnp.where(low, vo, swap(tb_))
+        sg[64 * b : 64 * b + 64, :] = silu(jnp.where(low, swap(vb), to_))
 
     rates = [rate_all[n : n + 1, :] for n in range(N)]
     zero_states = tuple(jnp.zeros((8, 128), F32) for _ in range(N))
@@ -224,7 +200,7 @@
 
     def row_body(i, states):
         rows = [pl.multiple_of(i * 64 + 8 * u, 8) for u in range(8)]
-        return scan_block(states, rows, step, x2, bc, rows, rates, put)
+        return scan_block(states, rows, rows, step, x2, bc, rates, put)
 
     lax.fori_loop(0, C, row_body, zero_states)
 
@@ -248,16 +224,6 @@
     @pl.when(r > 0)
     def _():
         up.start()
-
-    @sent.append
-    def _():
-        @pl.when(r < R - 1)
-        def _():
-            down.wait_send()
-
-        @pl.when(r > 0)
-        def _():
-            up.wait_send()
 
     sub = lax.broadcasted_iota(jnp.int32, (8, 128), 0)
 
@@ -271,6 +237,8 @@
             below = jnp.where(sub == 7, 0.0, pltpu.roll(q[2], 7, 0))
             acc[pl.ds(pl.multiple_of(b * 64 + 8 * u, 8), 8), :] = conv_bias + above + q[1] + below
 
+    every("col", sx, pp_s, px_r).wait_send()
+    every("col", sx, px_s, px_r).wait_send()
     @pl.when(r == 0)
     def _():
         rh[0] = jnp.zeros((TW, 128), BF16)
@@ -302,62 +270,46 @@
         s3[b] = jnp.where(low, near, far).astype(BF16)
         s3[C - 1 - b] = jnp.where(low, far, near).astype(BF16)
 
-    to_col(s3, r3, m_s, m_r, False)
-
+    send("col", s3, r3, m_s, m_r, False)
     r3[c] = s3[c]
-
-    @pl.loop(0, C)
-    def _(s):
-        @pl.when(s != c)
-        def _():
-            col_copy(s3, r3, m_s.at[s], m_r.at[s], s, s, s).wait_recv()
-
-    total = jnp.zeros((64, 128), F32)
+    every("col", r3, m_s, m_r).wait_recv()
+
     for j in range(R):
         one, two = r3[2 * j].astype(F32), r3[2 * j + 1].astype(F32)
-        first = jnp.where(low, one, swap(two))
-        second = jnp.where(low, swap(one), two)
-        tokens = jnp.concatenate([first, turn(second)], axis=0).astype(BF16)
-        tokens = dot(perm, tokens).astype(BF16)
-        s4[j] = tokens
-        total = total + dot(tokens, wcp_ref[128 * j : 128 * j + 128, :])
-    rp4[r] = total.astype(BF16)
-
-    to_row(rp4, rp4, q_s, q_r, True)
-
-    to_row(s4, r4, c_s, c_r, False)
-
+        tok[0:32, 128 * j : 128 * j + 128] = jnp.where(low, one, swap(two)).astype(BF16)
+        tok[32:64, 128 * j : 128 * j + 128] = turn(jnp.where(low, swap(one), two)).astype(BF16)
+    rp4[r] = dot(perm, dot(tok[...], wcp_ref[...]).astype(BF16)).astype(BF16)
+    send("row", rp4, rp4, q_s, q_r, True)
+    for j in range(R):
+        s4[j] = dot(perm, tok[:, 128 * j : 128 * j + 128]).astype(BF16)
+    send("row", s4, r4, c_s, c_r, False)
     r4[r] = s4[r]
+    every("col", s3, m_s, m_r).wait_send()
+
+    @pl.when(r < R - 1)
+    def _():
+        down.wait_send()
+
+    @pl.when(r > 0)
+    def _():
+        up.wait_send()
 
     HT = 64 * R
 
-    @pl.loop(0, R)
-    def _(k):
-        s = lax.rem(r + k, R)
-
-        @pl.when(s != r)
-        def _():
-            row_copy(rp4, rp4, q_s.at[s], q_r.at[s], s, s, s).wait_recv()
-
-        src = rp4[s]
+    every("row", rp4, q_s, q_r).wait_recv()
+    src4 = rp4[...].reshape(HT, 128)
+    for d in range(2):
+        raw = dot(src4, wd_ref[:, 128 + 128 * d : 256 + 128 * d])
+        step[d * HT : d * HT + HT, :] = softplus(raw + biasc[d : d + 1, :])
+
+    @pl.loop(0, 8)
+    def _(q):
+        at = pl.ds(pl.multiple_of(q * 512, 512), 512)
         for d in range(2):
-            rows = pl.ds(pl.multiple_of(d * HT + s * 64, 64), 64)
-            raw = dot(src, wd_ref[:, 128 + 128 * d : 256 + 128 * d])
-            step[rows, :] = softplus(raw + biasc[d : d + 1, :])
-            for q in range(8):
-                bc[rows, q * 512 : q * 512 + 512] = dot(src, sel[1 + d, :, q * 512 : q * 512 + 512])
-
-    @pl.loop(0, R)
-    def _(k):
-        s = lax.rem(r + k, R)
-
-        @pl.when(s != r)
-        def _():
-            row_copy(s4, r4, c_s.at[s], c_r.at[s], s, s, s).wait_recv()
-
-        cells = r4[s].astype(F32)
-        for d in range(2):
-            x2[pl.ds(pl.multiple_of(d * HT + s * 64, 64), 64), :] = cells
+            bc[d * HT : d * HT + HT, at] = dot(rp4[...].reshape(HT, 128), sel[1 + d, :, at])
+
+    every("row", r4, c_s, c_r).wait_recv()
+    x2[0:HT, :] = r4[...].reshape(HT, 128).astype(F32)
 
     for d in range(2):
         rate_d = ratec[d] * -LOG2E
@@ -367,7 +319,8 @@
             block = i if d == 0 else R - 1 - i
             order = range(8) if d == 0 else range(7, -1, -1)
             rows = [pl.multiple_of(d * HT + block * 64 + 8 * u, 8) for u in order]
-            return scan_block(states, rows, step, x2, bc, rows, rates_d, put)
+            x_rows = [pl.multiple_of(block * 64 + 8 * u, 8) for u in order]
+            return scan_block(states, rows, x_rows, step, x2, bc, rates_d, put)
 
         lax.fori_loop(0, R, col_body, zero_states)
 
@@ -375,7 +328,8 @@
         out_ref[64 * b : 64 * b + 64, :] = (
             y2[64 * b : 64 * b + 64, :] + y2[HT + 64 * b : HT + 64 * b + 64, :]).astype(BF16)
 
-    finish()
+    every("row", s4, q_s, q_r).wait_send()
+    every("row", s4, c_s, c_r).wait_send()
 
 
 def local(R, C, features, gate_branch, w_row_proj, w_dt_row, dt_bias_row, rate_row, skip_row,
@@ -411,6 +365,7 @@
             pltpu.VMEM((2, TW, 128), BF16),
             pltpu.VMEM((C, 32, 128), BF16),
             pltpu.VMEM((C, 32, 128), BF16),
+            pltpu.VMEM((64, E), BF16),
             pltpu.VMEM((R, 64, 128), BF16),
             pltpu.VMEM((R, 64, 128), BF16),
             pltpu.VMEM((R, 64, 128), BF16),
@@ -423,14 +378,15 @@
             pltpu.VMEM((32 * C + 16, 128), F32),
             pltpu.VMEM((32 * C, 128), F32),
             pltpu.VMEM((TW + 16, 128), F32),
-            dma((C,)), dma((C,)), dma((C,)), dma((C,)), dma((2,)), dma((2,)),
-            dma((C,)), dma((C,)), dma((R,)), dma((R,)), dma((R,)), dma((R,)),
+            dma, dma, dma, dma((C,)), dma((2,)), dma((2,)), dma, dma, dma, dma, dma, dma,
         ],
         compiler_params=pltpu.CompilerParams(
-            collective_id=0, has_side_effects=True, vmem_limit_bytes=63 << 20),
-    )(features.reshape(64, E), gate_branch.reshape(64, E), w_row_proj, w_dt_row, dt_bias_row,
-      jnp.transpose(rate_row, (0, 2, 1)), skip_row.reshape(1, 64), conv_kernel,
-      conv_bias.reshape(1, 64), w_col_proj, w_dt_col, dt_bias_col, jnp.transpose(rate_col, (0, 2, 1)))
+            collective_id=0, has_side_effects=True, vmem_limit_bytes=40 << 20),
+    )(*(pltpu.with_memory_space_constraint(v, pltpu.HBM) for v in (
+        features.reshape(64, E), gate_branch.reshape(64, E), w_row_proj, w_dt_row, dt_bias_row,
+        jnp.transpose(rate_row, (0, 2, 1)), skip_row.reshape(1, 64), conv_kernel,
+        conv_bias.reshape(1, 64), w_col_proj, w_dt_col, dt_bias_col,
+        jnp.transpose(rate_col, (0, 2, 1)))))
     return out.reshape(8 * R, 8, 128)
 
 

time: 41.8 us -> 40.3 us (0.964)
  local copies, waits for them, and re-layouts: 1.57 us -> 0.66 us
  Pallas kernels: 40.1 us -> 39.5 us
    unnamed x1, local copies, waits for them, and re-layouts: 1.57 us -> 0.66 us
    pallas_call x1, Pallas kernels: 40.1 us -> 39.5 us  [local(): pl.pallas_call(functools.partial(kernel, R, C), out_shape=jax.ShapeDtypeS...]
where the time goes in v2:
time: 40.3 us; the launch traced here: 40.2 us
  Pallas kernels  39.5 us (98%)
  local copies, waits for them, and re-layouts  0.66 us (2%)
    pallas_call x1, Pallas kernels, local(): pl.pallas_call(functools.partial(kernel, R, C), out_shape=jax.ShapeDtypeS...  39.5 us

profile of v2, /device:TPU:0, one launch (start us, length us, event | category | flops | bytes accessed | tf_op | source)
XLA Modules:
  0.0 40.2 jit_solution(3612123566372091050)
XLA Ops:
  0.0 39.5 %shard_map.127 = bf16[512,128]{1,0:T(8,128)(2,1)S(1)} custom-call(bf16[64,1024]{1,0:T(8,128)(2,1)} %bitcast.8, bf16[64,1024]{1,0:T(8,128)(2,1)} %bitcast.9, bf16[1024,128]{1,0:T(8,128)(2,1)} %wrp_hbm.1, bf16[2,32,64]{2,1,0:T(8,128)(2,1)} %wdtr_hbm.1, f32[2,64]{1,0:T(2,128)} %biasr_hbm.1, f32[2,16,64]{2,1,0:T(8,128)} %bitcast.10, f32[1,64]{1,0:T(1,128)} %bitcast.12, ...), custom_call_target="tpu_custom_call" | custom-call | tf_op jit(solution)/shard_map/pallas_call | solution.py:340
  39.5 0.7 %copy.15 = bf16[64,8,128]{2,1,0:T(8,128)(2,1)} copy(bf16[64,8,128]{2,1,0:T(8,128)(2,1)S(1)} %bitcast.7) | data formatting | bytes 262144

commit v3 on v2

--- a/solution.py
+++ b/solution.py
@@ -56,9 +56,9 @@
     out_ref,
     f_ref, g_ref, wrp_ref, wdtr, biasr, rater, skipr, kern, biask, wcp_ref, wdtc, biasc, ratec,
     wd_ref, load_sem,
-    sx, rx, rp, sh, rh, s3, r3, tok, s4, r4, rp4,
-    sel, bc, step, x2, y2, sg, z, acc, hz,
-    px_s, px_r, pp_s, pp_r, h_s, h_r, m_s, m_r, c_s, c_r, q_s, q_r,
+    sx, rx, sgx, rg, rp, sh, rh, s3, r3, s4, r4, rp4,
+    sel, bc, step, x2, y2, lay, z, acc, hz,
+    px_s, px_r, pg_s, pg_r, pp_s, pp_r, h_s, h_r, m_s, m_r, c_s, c_r, q_s, q_r,
 ):
     r, c = lax.axis_index("row"), lax.axis_index("col")
     half = C // 2
@@ -113,24 +113,32 @@
     tb = lax.broadcasted_iota(jnp.int32, (64, 64), 1)
     perm = jnp.where(tb == lax.rem(ta, 8) * 8 + lax.div(ta, 8), 1.0, 0.0).astype(BF16)
 
+    def packed(v):
+        near, far = v[0:32, :], turn(v[32:64, :])
+        return jnp.where(low, near, swap(far)).astype(BF16), jnp.where(low, swap(near), far).astype(BF16)
+
     loads[0].wait()
     loads[1].wait()
-    proj = dot(f_ref[...], wrp_ref[...]).astype(BF16)
-    rp[c] = dot(perm, proj).astype(BF16)
-
-    loads[2].wait()
+    proj = dot(f_ref[...], wrp_ref[...]).astype(BF16).astype(F32)
+    for h in range(8):
+        lay[pl.ds(h, 8, stride=8), :] = proj[8 * h : 8 * h + 8, :]
+    rp[c] = lay[...].astype(BF16)
+    turned = dot(perm, f_ref[...])
     for j in range(half):
-        fj = dot(perm, f_ref[:, 128 * j : 128 * j + 128])
-        gj = dot(perm, g_ref[:, 128 * j : 128 * j + 128])
-        sx[2 * j] = jnp.where(low, fj, swap(gj)).astype(BF16)
-        sx[2 * j + 1] = jnp.where(low, swap(fj), gj).astype(BF16)
+        sx[2 * j], sx[2 * j + 1] = packed(turned[:, 128 * j : 128 * j + 128])
 
     pl.semaphore_wait(barrier, C - 1 + R - 1)
     for k in range(1, C):
         to = lax.rem(c + k, C)
         col_copy(rp, rp, pp_s, pp_r.at[c], c, c, to).start()
     send("col", sx, rx, px_s, px_r, False)
+    loads[2].wait()
+    turned = dot(perm, g_ref[...])
+    for j in range(half):
+        sgx[2 * j], sgx[2 * j + 1] = packed(turned[:, 128 * j : 128 * j + 128])
+    send("col", sgx, rg, pg_s, pg_r, False)
     rx[c] = sx[c]
+    rg[c] = sgx[c]
 
     kk = lax.broadcasted_iota(jnp.int32, (128, 128), 0)
     ll = lax.broadcasted_iota(jnp.int32, (128, 128), 1)
@@ -183,14 +191,17 @@
             for i in range(4):
                 bc[rows[i], q * 512 : q * 512 + 512] = spread[64 * i : 64 * i + 64, :]
 
+    def facing(ref, b):
+        one, two = ref[b].astype(F32), ref[C - 1 - b].astype(F32)
+        p, q = jnp.where(low, one, two), jnp.where(low, two, one)
+        return p, turn(swap(q)), q, turn(swap(p))
+
     every("col", rx, px_s, px_r).wait_recv()
     for b in range(half):
         o = C - 1 - b
-        vb, vo = rx[b].astype(F32), rx[o].astype(F32)
-        tb_, to_ = turn(vb), turn(vo)
-        x2[64 * b : 64 * b + 64, :] = jnp.where(low, vb, swap(to_))
-        x2[64 * o : 64 * o + 64, :] = jnp.where(low, vo, swap(tb_))
-        sg[64 * b : 64 * b + 64, :] = silu(jnp.where(low, swap(vb), to_))
+        parts = facing(rx, b)
+        x2[64 * b : 64 * b + 32, :], x2[64 * b + 32 : 64 * b + 64, :] = parts[0], parts[1]
+        x2[64 * o : 64 * o + 32, :], x2[64 * o + 32 : 64 * o + 64, :] = parts[2], parts[3]
 
     rates = [rate_all[n : n + 1, :] for n in range(N)]
     zero_states = tuple(jnp.zeros((8, 128), F32) for _ in range(N))
@@ -204,11 +215,13 @@
 
     lax.fori_loop(0, C, row_body, zero_states)
 
+    every("col", rg, pg_s, pg_r).wait_recv()
     z[0:8, :] = jnp.zeros((8, 128), F32)
     for b in range(half):
         here, there = slice(64 * b, 64 * b + 64), slice(64 * (C - 1 - b), 64 * (C - b))
         mix = skip * x2[here, :] + y2[here, :] + swap(turn(y2[there, :]))
-        gated = (mix * sg[here, :]).astype(BF16).astype(F32)
+        gate = jnp.concatenate(facing(rg, b)[:2], axis=0)
+        gated = (mix * silu(gate)).astype(BF16).astype(F32)
         z[64 * b + 8 : 64 * b + 72, :] = gated
     z[8 * TW + 8 : 8 * TW + 16, :] = swap(z[8 * TW : 8 * TW + 8, :])
 
@@ -237,8 +250,9 @@
             below = jnp.where(sub == 7, 0.0, pltpu.roll(q[2], 7, 0))
             acc[pl.ds(pl.multiple_of(b * 64 + 8 * u, 8), 8), :] = conv_bias + above + q[1] + below
 
-    every("col", sx, pp_s, px_r).wait_send()
+    every("col", rp, pp_s, px_r).wait_send()
     every("col", sx, px_s, px_r).wait_send()
+    every("col", sgx, pg_s, pg_r).wait_send()
     @pl.when(r == 0)
     def _():
         rh[0] = jnp.zeros((TW, 128), BF16)
@@ -274,14 +288,17 @@
     r3[c] = s3[c]
     every("col", r3, m_s, m_r).wait_recv()
 
+    tokens = []
     for j in range(R):
         one, two = r3[2 * j].astype(F32), r3[2 * j + 1].astype(F32)
-        tok[0:32, 128 * j : 128 * j + 128] = jnp.where(low, one, swap(two)).astype(BF16)
-        tok[32:64, 128 * j : 128 * j + 128] = turn(jnp.where(low, swap(one), two)).astype(BF16)
-    rp4[r] = dot(perm, dot(tok[...], wcp_ref[...]).astype(BF16)).astype(BF16)
+        tokens.append(jnp.concatenate(
+            [jnp.where(low, one, swap(two)), turn(jnp.where(low, swap(one), two))], axis=0).astype(BF16))
+        s4[j] = tokens[j]
+    proj = dot(jnp.concatenate(tokens, axis=1), wcp_ref[...]).astype(BF16).astype(F32)
+    for w in range(8):
+        lay[pl.ds(w, 8, stride=8), :] = proj[8 * w : 8 * w + 8, :]
+    rp4[r] = lay[...].astype(BF16)
     send("row", rp4, rp4, q_s, q_r, True)
-    for j in range(R):
-        s4[j] = dot(perm, tok[:, 128 * j : 128 * j + 128]).astype(BF16)
     send("row", s4, r4, c_s, c_r, False)
     r4[r] = s4[r]
     every("col", s3, m_s, m_r).wait_send()
@@ -309,7 +326,10 @@
             bc[d * HT : d * HT + HT, at] = dot(rp4[...].reshape(HT, 128), sel[1 + d, :, at])
 
     every("row", r4, c_s, c_r).wait_recv()
-    x2[0:HT, :] = r4[...].reshape(HT, 128).astype(F32)
+    for s in range(R):
+        cells = r4[s].astype(F32)
+        for w in range(8):
+            x2[pl.ds(64 * s + w, 8, stride=8), :] = cells[8 * w : 8 * w + 8, :]
 
     for d in range(2):
         rate_d = ratec[d] * -LOG2E
@@ -358,14 +378,15 @@
             pltpu.VMEM((2, N, 128), F32),
             pltpu.VMEM((128, 384), BF16),
             dma((13,)),
-            pltpu.VMEM((C, 64, 128), BF16),
-            pltpu.VMEM((C, 64, 128), BF16),
+            pltpu.VMEM((C, 32, 128), BF16),
+            pltpu.VMEM((C, 32, 128), BF16),
+            pltpu.VMEM((C, 32, 128), BF16),
+            pltpu.VMEM((C, 32, 128), BF16),
             pltpu.VMEM((C, 64, 128), BF16),
             pltpu.VMEM((2, TW, 128), BF16),
             pltpu.VMEM((2, TW, 128), BF16),
             pltpu.VMEM((C, 32, 128), BF16),
             pltpu.VMEM((C, 32, 128), BF16),
-            pltpu.VMEM((64, E), BF16),
             pltpu.VMEM((R, 64, 128), BF16),
             pltpu.VMEM((R, 64, 128), BF16),
             pltpu.VMEM((R, 64, 128), BF16),
@@ -374,11 +395,11 @@
             pltpu.VMEM((64 * C, 128), F32),
             pltpu.VMEM((64 * C, 128), F32),
             pltpu.VMEM((64 * C, 128), F32),
-            pltpu.VMEM((32 * C, 128), F32),
+            pltpu.VMEM((64, 128), F32),
             pltpu.VMEM((32 * C + 16, 128), F32),
             pltpu.VMEM((32 * C, 128), F32),
             pltpu.VMEM((TW + 16, 128), F32),
-            dma, dma, dma, dma((C,)), dma((2,)), dma((2,)), dma, dma, dma, dma, dma, dma,
+            dma, dma, dma, dma, dma, dma((C,)), dma((2,)), dma((2,)), dma, dma, dma, dma, dma, dma,
         ],
         compiler_params=pltpu.CompilerParams(
             collective_id=0, has_side_effects=True, vmem_limit_bytes=40 << 20),

time: 40.3 us -> 40.1 us (level)
  no operation moved by 1% of the time
where the time goes in v3:
time: 40.1 us; the launch traced here: 40 us
  Pallas kernels  39.4 us (98%)
  local copies, waits for them, and re-layouts  0.66 us (2%)
    pallas_call x1, Pallas kernels, local(): pl.pallas_call(functools.partial(kernel, R, C), out_shape=jax.ShapeDtypeS...  39.4 us

profile of v3, /device:TPU:0, one launch (start us, length us, event | category | flops | bytes accessed | tf_op | source)
XLA Modules:
  0.0 40.0 jit_solution(6262040125449382773)
XLA Ops:
  0.0 39.4 %shard_map.127 = bf16[512,128]{1,0:T(8,128)(2,1)S(1)} custom-call(bf16[64,1024]{1,0:T(8,128)(2,1)} %bitcast.8, bf16[64,1024]{1,0:T(8,128)(2,1)} %bitcast.9, bf16[1024,128]{1,0:T(8,128)(2,1)} %wrp_hbm.1, bf16[2,32,64]{2,1,0:T(8,128)(2,1)} %wdtr_hbm.1, f32[2,64]{1,0:T(2,128)} %biasr_hbm.1, f32[2,16,64]{2,1,0:T(8,128)} %bitcast.10, f32[1,64]{1,0:T(1,128)} %bitcast.12, ...), custom_call_target="tpu_custom_call" | custom-call | tf_op jit(solution)/shard_map/pallas_call | solution.py:360
  39.4 0.7 %copy.15 = bf16[64,8,128]{2,1,0:T(8,128)(2,1)} copy(bf16[64,8,128]{2,1,0:T(8,128)(2,1)S(1)} %bitcast.7) | data formatting | bytes 262144

commit v4 on v3

--- a/solution.py
+++ b/solution.py
@@ -56,12 +56,13 @@
     out_ref,
     f_ref, g_ref, wrp_ref, wdtr, biasr, rater, skipr, kern, biask, wcp_ref, wdtc, biasc, ratec,
     wd_ref, load_sem,
-    sx, rx, sgx, rg, rp, sh, rh, s3, r3, s4, r4, rp4,
+    sx, rx, sgx, rg, rp, srcs, sh, rh, s3, r3, s4, r4, rp4,
     sel, bc, step, x2, y2, lay, z, acc, hz,
-    px_s, px_r, pg_s, pg_r, pp_s, pp_r, h_s, h_r, m_s, m_r, c_s, c_r, q_s, q_r,
+    px_s, px_r, pg_s, pg_r, pp_s, pp_r, pf_s, pf_r, h_s, h_r, m_s, m_r, c_s, c_r, q_s, q_r,
 ):
     r, c = lax.axis_index("row"), lax.axis_index("col")
     half = C // 2
+    chip, core = lax.div(c, 2), lax.rem(c, 2)
     TW = half * 8
     lane = lax.broadcasted_iota(jnp.int32, (1, 128), 1)
     low = lane < 64
@@ -122,15 +123,16 @@
     proj = dot(f_ref[...], wrp_ref[...]).astype(BF16).astype(F32)
     for h in range(8):
         lay[pl.ds(h, 8, stride=8), :] = proj[8 * h : 8 * h + 8, :]
-    rp[c] = lay[...].astype(BF16)
+    rp[core, chip] = lay[...].astype(BF16)
     turned = dot(perm, f_ref[...])
     for j in range(half):
         sx[2 * j], sx[2 * j + 1] = packed(turned[:, 128 * j : 128 * j + 128])
 
     pl.semaphore_wait(barrier, C - 1 + R - 1)
-    for k in range(1, C):
-        to = lax.rem(c + k, C)
-        col_copy(rp, rp, pp_s, pp_r.at[c], c, c, to).start()
+    for k in range(1, half):
+        pltpu.make_async_remote_copy(
+            src_ref=rp.at[core, chip], dst_ref=rp.at[core, chip], send_sem=pp_s, recv_sem=pp_r,
+            device_id={"col": lax.rem(c + 2 * k, C)}, device_id_type=MESH).start()
     send("col", sx, rx, px_s, px_r, False)
     loads[2].wait()
     turned = dot(perm, g_ref[...])
@@ -168,28 +170,26 @@
     taps = [[beside(kern[i, j : j + 1, :], kern[i, 2 - j : 3 - j, :]) for j in range(3)] for i in range(3)]
     rate_all = beside(rater[0], rater[1]) * -LOG2E
 
-    base = jnp.where(c < half, c, C - 1 - c)
-    first = lax.div(base, 2)
-
-    @pl.loop(0, half // 2)
-    def _(k):
-        b = lax.rem(first + k, half // 2) * 2
-        blocks = (b, b + 1, C - 2 - b, C - 1 - b)
-        for s in blocks:
-            @pl.when(s != c)
-            def _():
-                col_copy(rp, rp, pp_s, pp_r.at[s], s, s, s).wait_recv()
-        projs = [rp[s].astype(F32) for s in blocks]
-        src = jnp.concatenate(
-            [jnp.where(low, projs[i], turn(projs[3 - i])) for i in range(4)], axis=0).astype(BF16)
-        rows = [pl.ds(pl.multiple_of(s * 64, 64), 64) for s in blocks]
-        steps = softplus(dot(src, wd_ref[:, 0:128]) + bias_row)
-        for i in range(4):
-            step[rows[i], :] = steps[64 * i : 64 * i + 64, :]
-        for q in range(8):
-            spread = dot(src, sel[0, :, q * 512 : q * 512 + 512])
-            for i in range(4):
-                bc[rows[i], q * 512 : q * 512 + 512] = spread[64 * i : 64 * i + 64, :]
+    direct = rp.at[core, pl.ds(0, half - 1)]
+    peers = pltpu.make_async_remote_copy(
+        src_ref=direct, dst_ref=direct, send_sem=pp_s, recv_sem=pp_r,
+        device_id={"col": c + 1 - 2 * core}, device_id_type=MESH)
+    peers.wait_recv()
+    passed = pltpu.make_async_remote_copy(
+        src_ref=rp.at[core], dst_ref=rp.at[core], send_sem=pf_s, recv_sem=pf_r,
+        device_id={"col": c + 1 - 2 * core}, device_id_type=MESH)
+    passed.start()
+    passed.wait_recv()
+    for b in range(half):
+        o = C - 1 - b
+        pb, po = rp[b % 2, b // 2].astype(F32), rp[o % 2, o // 2].astype(F32)
+        srcs[64 * b : 64 * b + 64, :] = jnp.where(low, pb, turn(po)).astype(BF16)
+        srcs[64 * o : 64 * o + 64, :] = jnp.where(low, po, turn(pb)).astype(BF16)
+    step[...] = softplus(dot(srcs[...], wd_ref[:, 0:128]) + bias_row)
+
+    for q in range(8):
+        at = slice(q * 512, q * 512 + 512)
+        bc[:, at] = dot(srcs[...], sel[0, :, at])
 
     def facing(ref, b):
         one, two = ref[b].astype(F32), ref[C - 1 - b].astype(F32)
@@ -210,10 +210,10 @@
         y2[pl.ds(row, 8), :] = out
 
     def row_body(i, states):
-        rows = [pl.multiple_of(i * 64 + 8 * u, 8) for u in range(8)]
+        rows = [pl.multiple_of(i * 128 + 8 * u, 8) for u in range(16)]
         return scan_block(states, rows, rows, step, x2, bc, rates, put)
 
-    lax.fori_loop(0, C, row_body, zero_states)
+    lax.fori_loop(0, C // 2, row_body, zero_states)
 
     every("col", rg, pg_s, pg_r).wait_recv()
     z[0:8, :] = jnp.zeros((8, 128), F32)
@@ -250,7 +250,8 @@
             below = jnp.where(sub == 7, 0.0, pltpu.roll(q[2], 7, 0))
             acc[pl.ds(pl.multiple_of(b * 64 + 8 * u, 8), 8), :] = conv_bias + above + q[1] + below
 
-    every("col", rp, pp_s, px_r).wait_send()
+    peers.wait_send()
+    passed.wait_send()
     every("col", sx, px_s, px_r).wait_send()
     every("col", sgx, pg_s, pg_r).wait_send()
     @pl.when(r == 0)
@@ -319,11 +320,10 @@
         raw = dot(src4, wd_ref[:, 128 + 128 * d : 256 + 128 * d])
         step[d * HT : d * HT + HT, :] = softplus(raw + biasc[d : d + 1, :])
 
-    @pl.loop(0, 8)
-    def _(q):
-        at = pl.ds(pl.multiple_of(q * 512, 512), 512)
-        for d in range(2):
-            bc[d * HT : d * HT + HT, at] = dot(rp4[...].reshape(HT, 128), sel[1 + d, :, at])
+    for d in range(2):
+        for q in range(8):
+            at = slice(q * 512, q * 512 + 512)
+            bc[d * HT : d * HT + HT, at] = dot(src4, sel[1 + d, :, at])
 
     every("row", r4, c_s, c_r).wait_recv()
     for s in range(R):
@@ -336,13 +336,13 @@
         rates_d = [rate_d[n : n + 1, :] for n in range(N)]
 
         def col_body(i, states):
-            block = i if d == 0 else R - 1 - i
-            order = range(8) if d == 0 else range(7, -1, -1)
-            rows = [pl.multiple_of(d * HT + block * 64 + 8 * u, 8) for u in order]
-            x_rows = [pl.multiple_of(block * 64 + 8 * u, 8) for u in order]
+            block = i if d == 0 else R // 2 - 1 - i
+            order = range(16) if d == 0 else range(15, -1, -1)
+            rows = [pl.multiple_of(d * HT + block * 128 + 8 * u, 8) for u in order]
+            x_rows = [pl.multiple_of(block * 128 + 8 * u, 8) for u in order]
             return scan_block(states, rows, x_rows, step, x2, bc, rates_d, put)
 
-        lax.fori_loop(0, R, col_body, zero_states)
+        lax.fori_loop(0, R // 2, col_body, zero_states)
 
     for b in range(R):
         out_ref[64 * b : 64 * b + 64, :] = (
@@ -382,7 +382,8 @@
             pltpu.VMEM((C, 32, 128), BF16),
             pltpu.VMEM((C, 32, 128), BF16),
             pltpu.VMEM((C, 32, 128), BF16),
-            pltpu.VMEM((C, 64, 128), BF16),
+            pltpu.VMEM((2, C // 2, 64, 128), BF16),
+            pltpu.VMEM((64 * C, 128), BF16),
             pltpu.VMEM((2, TW, 128), BF16),
             pltpu.VMEM((2, TW, 128), BF16),
             pltpu.VMEM((C, 32, 128), BF16),
@@ -399,7 +400,7 @@
             pltpu.VMEM((32 * C + 16, 128), F32),
             pltpu.VMEM((32 * C, 128), F32),
             pltpu.VMEM((TW + 16, 128), F32),
-            dma, dma, dma, dma, dma, dma((C,)), dma((2,)), dma((2,)), dma, dma, dma, dma, dma, dma,
+            dma, dma, dma, dma, dma, dma, dma, dma, dma((2,)), dma((2,)), dma, dma, dma, dma, dma, dma,
         ],
         compiler_params=pltpu.CompilerParams(
             collective_id=0, has_side_effects=True, vmem_limit_bytes=40 << 20),

time: 40.1 us -> 37.9 us (0.945)
  Pallas kernels: 39.4 us -> 37.1 us
    pallas_call x1, Pallas kernels: 39.4 us -> 37.1 us  [local(): pl.pallas_call(functools.partial(kernel, R, C), out_shape=jax.ShapeDtypeS...]
where the time goes in v4:
time: 37.9 us; the launch traced here: 37.8 us
  Pallas kernels  37.1 us (98%)
  local copies, waits for them, and re-layouts  0.66 us (2%)
    pallas_call x1, Pallas kernels, local(): pl.pallas_call(functools.partial(kernel, R, C), out_shape=jax.ShapeDtypeS...  37.1 us

profile of v4, /device:TPU:0, one launch (start us, length us, event | category | flops | bytes accessed | tf_op | source)
XLA Modules:
  0.0 37.8 jit_solution(9667883820880822264)
XLA Ops:
  0.0 37.1 %shard_map.127 = bf16[512,128]{1,0:T(8,128)(2,1)S(1)} custom-call(bf16[64,1024]{1,0:T(8,128)(2,1)} %bitcast.8, bf16[64,1024]{1,0:T(8,128)(2,1)} %bitcast.9, bf16[1024,128]{1,0:T(8,128)(2,1)} %wrp_hbm.1, bf16[2,32,64]{2,1,0:T(8,128)(2,1)} %wdtr_hbm.1, f32[2,64]{1,0:T(2,128)} %biasr_hbm.1, f32[2,16,64]{2,1,0:T(8,128)} %bitcast.10, f32[1,64]{1,0:T(1,128)} %bitcast.12, ...), custom_call_target="tpu_custom_call" | custom-call | tf_op jit(solution)/shard_map/pallas_call | solution.py:360
  37.1 0.7 %copy.15 = bf16[64,8,128]{2,1,0:T(8,128)(2,1)} copy(bf16[64,8,128]{2,1,0:T(8,128)(2,1)S(1)} %bitcast.7) | data formatting | bytes 262144

commit v5 on v4

--- a/solution.py
+++ b/solution.py
@@ -138,7 +138,6 @@
     turned = dot(perm, g_ref[...])
     for j in range(half):
         sgx[2 * j], sgx[2 * j + 1] = packed(turned[:, 128 * j : 128 * j + 128])
-    send("col", sgx, rg, pg_s, pg_r, False)
     rx[c] = sx[c]
     rg[c] = sgx[c]
 
@@ -179,6 +178,7 @@
         src_ref=rp.at[core], dst_ref=rp.at[core], send_sem=pf_s, recv_sem=pf_r,
         device_id={"col": c + 1 - 2 * core}, device_id_type=MESH)
     passed.start()
+    send("col", sgx, rg, pg_s, pg_r, False)
     passed.wait_recv()
     for b in range(half):
         o = C - 1 - b

time: 37.9 us -> 37.8 us (level)
  no operation moved by 1% of the time
where the time goes in v5:
time: 37.8 us; the launch traced here: 37.7 us
  Pallas kernels  37 us (98%)
  local copies, waits for them, and re-layouts  0.66 us (2%)
    pallas_call x1, Pallas kernels, local(): pl.pallas_call(functools.partial(kernel, R, C), out_shape=jax.ShapeDtypeS...  37 us

profile of v5, /device:TPU:0, one launch (start us, length us, event | category | flops | bytes accessed | tf_op | source)
XLA Modules:
  0.0 37.7 jit_solution(5617586052519484857)
XLA Ops:
  0.0 37.0 %shard_map.127 = bf16[512,128]{1,0:T(8,128)(2,1)S(1)} custom-call(bf16[64,1024]{1,0:T(8,128)(2,1)} %bitcast.8, bf16[64,1024]{1,0:T(8,128)(2,1)} %bitcast.9, bf16[1024,128]{1,0:T(8,128)(2,1)} %wrp_hbm.1, bf16[2,32,64]{2,1,0:T(8,128)(2,1)} %wdtr_hbm.1, f32[2,64]{1,0:T(2,128)} %biasr_hbm.1, f32[2,16,64]{2,1,0:T(8,128)} %bitcast.10, f32[1,64]{1,0:T(1,128)} %bitcast.12, ...), custom_call_target="tpu_custom_call" | custom-call | tf_op jit(solution)/shard_map/pallas_call | solution.py:360
  37.0 0.7 %copy.15 = bf16[64,8,128]{2,1,0:T(8,128)(2,1)} copy(bf16[64,8,128]{2,1,0:T(8,128)(2,1)S(1)} %bitcast.7) | data formatting | bytes 262144
